TPU v7x, 32 devices: a whole 2x2x4 slice. The times are simulated.
32 devices in a mesh: rows: 8 (over z, x), cols: 4 (over y, core).
Axes of the slice: x: 2, y: 2, z: 4, core: 2. Of those that a mesh axis runs over, the one named last changes fastest.
Arguments:
- block_list: int32 [64, 24], P('rows', 'cols'), may hold values from -1 to 63, as said below
- points: bfloat16 [16, 16384], P(None, 'rows'), may hold values from -4 to 4
- targets: float32 [32, 16384], P(None, 'rows'), may hold values from -6 to 6
Outputs:
- solution: float32 [32, 16384], P(None, 'rows')
- residual: float32 [32, 16384], P(None, 'rows')
Inputs may be any that keep to these rules, and one draw needn't show every extreme that they name: `block_list`: A non-empty entry j of block row i satisfies j <= i. Within the 6 slots of a block row held by one index of cols, the entries lie in different groups of 8 consecutive blocks. Of all slots held by one device (8 block rows of 6 slots), at most 6 name blocks of any one group of 8 consecutive blocks, and in every draw some device reaches 6.
All inputs are finite; a program needn't handle non-finite values.
Results may differ from a plain program's by a relative error of at most 0.0057.
Values may be sent and summed in bfloat16 or wider, within the bound.
No kernel may reach another device: no remote copies, remote signals or barrier semaphores. Data moves between devices by JAX's collectives and lax.ppermute only.
A program may use at most 64 MiB of HBM per device.

v0:
```python
import jax
import jax.numpy as jnp
from jax import lax
from jax.sharding import PartitionSpec as P

ITERS = 2


REG = 1.5
RADIUS = 0.25


def wendland(left_x, right_x):
    left_f = left_x.astype(jnp.float32)
    right_f = right_x.astype(jnp.float32)
    left_sq = jnp.sum(left_f * left_f, axis=1)
    right_sq = jnp.sum(right_f * right_f, axis=1)
    inner_prod = jnp.einsum("nda,ndb->nab", left_f, right_f, precision=lax.Precision.HIGHEST)
    dist_sq = left_sq[:, :, None] + right_sq[:, None, :] - 2.0 * inner_prod
    scaled = jnp.sqrt(jnp.maximum(dist_sq, 0.0)) / RADIUS
    remain = jnp.maximum(1.0 - scaled, 0.0)
    square = remain * remain
    return square * square * (4.0 * scaled + 1.0)


def local(block_list, points, targets):
    row_count = lax.axis_size("rows")
    row_index = lax.axis_index("rows")
    block_rows, slot_width = block_list.shape
    coord_dim, npoints = points.shape
    outputs = targets.shape[0]
    block_len = npoints // block_rows
    slot_count = block_rows * slot_width
    capacity = (slot_count + row_count - 1) // row_count
    buffer_len = row_count * capacity
    turn_rows = 4
    turn_count = block_rows // turn_rows
    entries = block_list.reshape(slot_count)
    is_live = entries >= 0
    owners = jnp.where(is_live, entries // block_rows, 0)
    local_idx = jnp.where(is_live, entries - owners * block_rows, 0)
    first_row = row_index * block_rows
    row_global = first_row + jnp.arange(slot_count, dtype=jnp.int32) // slot_width
    off_diag = is_live & (entries != row_global)
    owner_hits = (
        (owners[:, None] == jnp.arange(row_count, dtype=jnp.int32)[None, :]) & is_live[:, None]
    ).astype(jnp.int32)
    slot_rank = jnp.sum((jnp.cumsum(owner_hits, axis=0) - owner_hits) * owner_hits, axis=1)
    place_at = jnp.where(is_live, owners * capacity + slot_rank, buffer_len)
    pick_at = jnp.minimum(place_at, buffer_len - 1)
    wanted = jnp.full((buffer_len,), -1, jnp.int32).at[place_at].set(local_idx, mode="drop")
    askers = jnp.full((buffer_len,), -1, jnp.int32).at[place_at].set(row_global, mode="drop")
    request = jnp.stack([wanted, askers], axis=1).reshape(row_count, capacity, 2)
    incoming = lax.all_to_all(request, "rows", split_axis=0, concat_axis=0, tiled=True).reshape(
        buffer_len, 2
    )
    in_live = incoming[:, 0] >= 0
    in_idx = jnp.maximum(incoming[:, 0], 0)
    collect_map = (
        (in_idx[None, :] == jnp.arange(block_rows, dtype=jnp.int32)[:, None]) & in_live[None, :]
    ).astype(jnp.float32)

    def serve(blocks):
        chosen = jnp.where(in_live[:, None, None], blocks[in_idx], jnp.zeros((), blocks.dtype))
        arrived = lax.all_to_all(
            chosen.reshape(row_count, capacity, blocks.shape[1], block_len),
            "rows",
            split_axis=0,
            concat_axis=0,
            tiled=True,
        )
        gotten = arrived.reshape(buffer_len, blocks.shape[1], block_len)[pick_at]
        return jnp.where(is_live[:, None, None], gotten, jnp.zeros((), gotten.dtype))

    def collect(terms):
        flat = terms.reshape(buffer_len, -1)
        summed = jnp.dot(
            collect_map, flat, precision=lax.Precision.HIGHEST, preferred_element_type=jnp.float32
        )
        return summed.reshape(block_rows, terms.shape[1], block_len)

    def give_back(mirror):
        placed = (
            jnp.zeros((buffer_len,) + mirror.shape[1:], jnp.float32)
            .at[place_at]
            .set(mirror, mode="drop")
        )
        arrived = lax.all_to_all(
            placed.reshape(row_count, capacity, mirror.shape[1], block_len),
            "rows",
            split_axis=0,
            concat_axis=0,
            tiled=True,
        )
        return collect(arrived.reshape(buffer_len, mirror.shape[1], block_len))

    def column_total(partial_value):
        return lax.psum(partial_value, "cols")

    def global_sum(values):
        return lax.psum(values, "rows")

    own_x = points.reshape(coord_dim, block_rows, block_len).transpose(1, 0, 2)
    far_x = serve(own_x)
    grouped_x = own_x.reshape(turn_count, turn_rows, coord_dim, block_len)
    grouped_far = far_x.reshape(turn_count, turn_rows * slot_width, coord_dim, block_len)
    grouped_live = is_live.reshape(turn_count, turn_rows * slot_width)
    grouped_off = off_diag.reshape(turn_count, turn_rows * slot_width)

    def row_pass(own_w, far_w):

        def row_step(pieces):
            near_x, remote_x, live_now, off_now = (pieces[0], pieces[1], pieces[2], pieces[3])
            values = jnp.where(
                live_now[:, None, None],
                wendland(jnp.repeat(near_x, slot_width, axis=0), remote_x),
                0.0,
            )
            if own_w is None:
                direct = jnp.sum(
                    jnp.sum(values, axis=2).reshape(turn_rows, slot_width, block_len), axis=1
                )[:, None, :]
                mirror = jnp.where(off_now[:, None], jnp.sum(values, axis=1), 0.0)[:, None, :]
                return (direct, mirror)
            kernel_bf = values.astype(jnp.bfloat16)
            direct = jnp.einsum(
                "nab,nob->noa", kernel_bf, pieces[5], preferred_element_type=jnp.float32
            )
            direct = jnp.sum(direct.reshape(turn_rows, slot_width, outputs, block_len), axis=1)
            mirror = jnp.einsum(
                "nab,noa->nob",
                kernel_bf,
                jnp.repeat(pieces[4], slot_width, axis=0),
                preferred_element_type=jnp.float32,
            )
            return (direct, jnp.where(off_now[:, None, None], mirror, 0.0))

        pieces = (grouped_x, grouped_far, grouped_live, grouped_off)
        if own_w is not None:
            pieces = pieces + (
                own_w.reshape(turn_count, turn_rows, outputs, block_len),
                far_w.reshape(turn_count, turn_rows * slot_width, outputs, block_len),
            )
        results = lax.map(row_step, pieces)
        channels = results[0].shape[2]
        direct = results[0].reshape(block_rows, channels, block_len)
        return (direct, results[1].reshape(slot_count, channels, block_len))

    direct, mirror = row_pass(None, None)
    degree_part = direct + give_back(mirror)
    inv_root = 1.0 / jnp.sqrt(1.0 + column_total(degree_part))
    resid = targets.reshape(outputs, block_rows, block_len).transpose(1, 0, 2)
    direction = resid
    solution = jnp.zeros_like(resid)
    norm_now = global_sum(jnp.sum(resid * resid, axis=(0, 2)))
    for iteration in range(ITERS):
        weights = (direction * inv_root).astype(jnp.bfloat16)
        apply_far_w = serve(weights)
        apply_direct, apply_mirror = row_pass(weights, apply_far_w)
        apply_partial_value = apply_direct + give_back(apply_mirror)
        applied = REG * direction + inv_root * column_total(apply_partial_value)
        step_size = norm_now / global_sum(jnp.sum(direction * applied, axis=(0, 2)))
        solution = solution + step_size[None, :, None] * direction
        resid = resid - step_size[None, :, None] * applied
        if iteration + 1 < ITERS:
            norm_next = global_sum(jnp.sum(resid * resid, axis=(0, 2)))
            direction = resid + (norm_next / norm_now)[None, :, None] * direction
            norm_now = norm_next
    return (
        solution.transpose(1, 0, 2).reshape(outputs, npoints),
        resid.transpose(1, 0, 2).reshape(outputs, npoints),
    )


def solution(mesh):
    placed = (P("rows", "cols"), P(None, "rows"), P(None, "rows"))
    return jax.shard_map(
        local,
        mesh=mesh,
        in_specs=placed,
        out_specs=(P(None, "rows"), P(None, "rows")),
        check_vma=False,
    )
```

profile of v0, /device:TPU:0, one launch (start us, length us, event | category | flops | bytes accessed | tf_op | source)
XLA Modules:
  0.0 374.2 jit_solution(17328673378696880646)
XLA Ops:
  11.4 7.3 %all-to-all-start = ((s32[8,6,2]{1,2,0:T(2,128)}), s32[8,6,2]{1,2,0:T(2,128)S(1)}, u32[]{:S(2)}, u32[]{:S(2)}) async-start(s32[8,6,2]{1,2,0:T(2,128)} %copy.20), calls=%async_computation | async-start | bytes 16384 | tf_op jit(solution)/shard_map/all_to_all | solution.py:54
  18.6 0.8 copy.76
  19.5 5.7 %all-to-all-done = s32[8,6,2]{1,2,0:T(2,128)S(1)} async-done(((s32[8,6,2]{1,2,0:T(2,128)}), s32[8,6,2]{1,2,0:T(2,128)S(1)}, u32[]{:S(2)}, u32[]{:S(2)}) %all-to-all-start) | async-done | bytes 416 | tf_op jit(solution)/shard_map/all_to_all | solution.py:54
  25.9 0.9 broadcast_select_fusion.5
  26.8 3.5 all-to-all-start.1
  31.1 9.6 %all-to-all-done.1 = bf16[8,6,16,256]{3,2,1,0:T(8,128)(2,1)S(1)} async-done(((bf16[8,6,16,256]{3,2,1,0:T(8,128)(2,1)}), bf16[8,6,16,256]{3,2,1,0:T(8,128)(2,1)S(1)}, u32[]{:S(2)}, u32[]{:S(2)}) %all-to-all-start.1) | async-done | bytes 393248 | tf_op jit(solution)/shard_map/all_to_all | solution.py:65
  41.4 12.5 %while.42 = (s32[]{:T(128)}, f32[2,4,1,256]{3,2,1,0:T(1,128)S(1)}, f32[2,24,1,256]{3,1,2,0:T(8,128)S(1)}, pred[2,24]{1,0:T(4,128)(4,1)S(1)}, bf16[2,4,16,256]{3,...) while((s32[]{:T(128)}, f32[2,4,1,256]{3,2,1,0:T(1,128)S(1)}, ...), condition=%wide.region_12.13_spmd, body=%wide.region_6.12_spmd.sunk | while | flops 74260480 | bytes 1274609 | solution.py:144
  41.6 5.8 %fusion.103 = (f32[24,256]{1,0:T(8,128)S(1)}, f32[24,256]{1,0:T(8,128)S(1)}) fusion(bf16[24,16,256]{2,1,0:T(8,128)(2,1)S(1)} %bitcast.309, bf16[2,24,16,256]{3,2,1,0:T(8,128)(2,1)S(1)} %get-tuple-element.664, s32[]{:T(128)} %get-tuple-element.650, f32[24,256]{1,0:T(8,128)S(1)} %multiply_reduce_fusion.15, f32[24,256]{1,0:T(8,128)S(1)} %add.332, ...), kind=kOutput, calls=%fused_computation.152.clone.1 | convolution fusion | flops 73912320 | bytes 492036 | tf_op jit(solution)/shard_map/while/body/eval_jaxpr/nda,ndb->nab/dot_general | solution.py:18
  47.9 5.9 %fusion.103 = (f32[24,256]{1,0:T(8,128)S(1)}, f32[24,256]{1,0:T(8,128)S(1)}) fusion(bf16[24,16,256]{2,1,0:T(8,128)(2,1)S(1)} %bitcast.309, bf16[2,24,16,256]{3,2,1,0:T(8,128)(2,1)S(1)} %get-tuple-element.664, s32[]{:T(128)} %get-tuple-element.650, f32[24,256]{1,0:T(8,128)S(1)} %multiply_reduce_fusion.15, f32[24,256]{1,0:T(8,128)S(1)} %add.332, ...), kind=kOutput, calls=%fused_computation.152.clone.1 | convolution fusion | flops 73912320 | bytes 492036 | tf_op jit(solution)/shard_map/while/body/eval_jaxpr/nda,ndb->nab/dot_general | solution.py:18
  55.4 3.7 all-to-all-start.2
  59.2 6.7 %all-to-all-done.2 = f32[8,6,1,256]{3,2,1,0:T(1,128)S(1)} async-done(((f32[8,6,1,256]{3,2,1,0:T(1,128)}), f32[8,6,1,256]{3,2,1,0:T(1,128)S(1)}, u32[]{:S(2)}, u32[]{:S(2)}) %all-to-all-start.2) | async-done | bytes 49184 | tf_op jit(solution)/shard_map/all_to_all | solution.py:88
  66.1 5.8 %psum.50 = f32[8,1,256]{2,0,1:T(8,128)S(1)} all-reduce(f32[8,1,256]{2,0,1:T(8,128)S(1)} %fusion.37), channel_id=1, replica_groups=mesh['rows'=8,'cols'=4] {'cols'}, use_global_device_ids=true, to_apply=%region_14.15 | all-reduce | flops 2048 | bytes 16384 | tf_op jit(solution)/shard_map/psum | solution.py:98
  72.6 1.0 broadcast_select_fusion.2
  73.6 3.5 all-to-all-start.3
  77.2 20.3 %all-to-all-done.3 = bf16[8,6,32,256]{3,2,1,0:T(8,128)(2,1)S(1)} async-done(((bf16[8,6,32,256]{3,2,1,0:T(8,128)(2,1)}), bf16[8,6,32,256]{3,2,1,0:T(8,128)(2,1)S(1)}, u32[]{:S(2)}, u32[]{:S(2)}) %all-to-all-start.3) | async-done | bytes 786464 | tf_op jit(solution)/shard_map/all_to_all | solution.py:65
  98.2 1.3 broadcast.414.clone
  99.6 16.1 %while.43 = (s32[]{:T(128)}, f32[2,4,32,256]{3,2,1,0:T(8,128)S(1)}, f32[2,24,32,256]{3,2,1,0:T(8,128)}, bf16[2,24,32,256]{3,2,1,0:T(8,128)(2,1)S(1)}, pred[2,24]...) while((s32[]{:T(128)}, f32[2,4,32,256]{3,2,1,0:T(8,128)S(1)}, ...), condition=%wide.region_19.20_spmd, body=%wide.region_15.19_spmd.sunk | while | flops 274375680 | bytes 14607621 | solution.py:144
  99.8 5.1 %select_convert_fusion.4 = bf16[24,256,256]{2,1,0:T(8,128)(2,1)S(1)} fusion(f32[24,256]{1,0:T(8,128)S(1)} %multiply_reduce_fusion.16, f32[24,256]{1,0:T(8,128)S(1)} %add.338, pred[24]{0:T(512)(128)(4,1)S(1)} %get-tuple-element.625, bf16[24,16,256]{2,1,0:T(8,128)(2,1)S(1)} %bitcast.310, bf16[2,24,16,256]{3,2,1,0:T(8,128)(2,1)S(1)} %get-tuple-element.696, ...), kind=kOutput, calls=%fused_computation.23.clone.1 | convolution fusion | flops 72351744 | bytes 3588612 | tf_op jit(solution)/shard_map/while/body/eval_jaxpr/nda,ndb->nab/dot_general | solution.py:18
  105.0 1.5 fusion.112
  106.5 1.0 fusion.111
  107.8 5.1 %select_convert_fusion.4 = bf16[24,256,256]{2,1,0:T(8,128)(2,1)S(1)} fusion(f32[24,256]{1,0:T(8,128)S(1)} %multiply_reduce_fusion.16, f32[24,256]{1,0:T(8,128)S(1)} %add.338, pred[24]{0:T(512)(128)(4,1)S(1)} %get-tuple-element.625, bf16[24,16,256]{2,1,0:T(8,128)(2,1)S(1)} %bitcast.310, bf16[2,24,16,256]{3,2,1,0:T(8,128)(2,1)S(1)} %get-tuple-element.696, ...), kind=kOutput, calls=%fused_computation.23.clone.1 | convolution fusion | flops 72351744 | bytes 3588612 | tf_op jit(solution)/shard_map/while/body/eval_jaxpr/nda,ndb->nab/dot_general | solution.py:18
  113.0 1.5 fusion.112
  114.6 1.0 fusion.111
  115.9 5.1 %scatter_fusion = f32[48,32,256]{2,1,0:T(8,128)S(1)} fusion(f32[48,32,256]{2,1,0:T(8,128)S(1)} %broadcast.415.clone, s32[48]{0:T(128)S(1)} %fusion.62, f32[48,32,256]{2,1,0:T(8,128)} %bitcast.47), kind=kCustom, calls=%fused_computation.9 | custom fusion | bytes 4718784 | tf_op jit(solution)/shard_map/scatter | solution.py:86
  121.0 40.5 %all_to_all.35 = f32[8,6,32,256]{3,2,1,0:T(8,128)S(1)} all-to-all(f32[8,6,32,256]{3,2,1,0:T(8,128)S(1)} %bitcast.302), channel_id=1, replica_groups=mesh['rows'=8,'cols'=4] {'rows'}, dimensions={0} | all-to-all | bytes 3145728 | tf_op jit(solution)/shard_map/all_to_all | solution.py:88
  161.5 2.2 fusion.31
  163.8 31.2 %all-reduce.4.cloned.1.call-done = f32[8,32,256]{2,0,1:T(8,128)} async-done(((f32[8,32,256]{2,0,1:T(8,128)}), f32[8,32,256]{2,0,1:T(8,128)}) %all-reduce.4.cloned.1.call-update) | async-done | bytes 262160 | tf_op jit(solution)/shard_map/psum | solution.py:98
  195.0 1.3 fusion.41
  196.3 21.4 %all-reduce = (f32[32]{0:T(128)S(1)}, f32[32]{0:T(128)S(1)}) all-reduce(f32[32]{0:T(128)S(1)} %get-tuple-element.383, f32[32]{0:T(128)S(1)} %get-tuple-element.382), channel_id=1, replica_groups=mesh['rows'=8,'cols'=4] {'rows'}, use_global_device_ids=true, to_apply=%region_1.2 | all-reduce | flops 64 | bytes 512 | tf_op jit(solution)/shard_map/psum | solution.py:101
  217.7 1.5 multiply_reduce_fusion.7
  219.1 17.2 %psum.53 = f32[32]{0:T(128)S(1)} all-reduce(f32[32]{0:T(128)S(1)} %multiply_reduce_fusion.7), channel_id=1, replica_groups=mesh['rows'=8,'cols'=4] {'rows'}, use_global_device_ids=true, to_apply=%region_25.26 | all-reduce | flops 32 | bytes 256 | tf_op jit(solution)/shard_map/psum | solution.py:101
  236.3 1.1 multiply_convert_fusion
  238.3 16.1 %all_to_all.37 = bf16[8,6,32,256]{3,2,1,0:T(8,128)(2,1)S(1)} all-to-all(bf16[8,6,32,256]{3,2,1,0:T(8,128)(2,1)S(1)} %broadcast_select_fusion.1), channel_id=1, replica_groups=mesh['rows'=8,'cols'=4] {'rows'}, dimensions={0} | all-to-all | bytes 1572864 | tf_op jit(solution)/shard_map/all_to_all | solution.py:65
  255.1 1.3 broadcast.414
  256.5 16.1 %while.44 = (s32[]{:T(128)}, f32[2,4,32,256]{3,2,1,0:T(8,128)S(1)}, f32[2,24,32,256]{3,2,1,0:T(8,128)}, bf16[2,24,32,256]{3,2,1,0:T(8,128)(2,1)S(1)}, pred[2,24]...) while((s32[]{:T(128)}, f32[2,4,32,256]{3,2,1,0:T(8,128)S(1)}, ...), condition=%wide.region_30.31_spmd, body=%wide.region_26.30_spmd.sunk | while | flops 274375680 | bytes 14607621 | solution.py:144
  256.7 5.1 %select_convert_fusion.5 = bf16[24,256,256]{2,1,0:T(8,128)(2,1)S(1)} fusion(f32[24,256]{1,0:T(8,128)S(1)} %multiply_reduce_fusion.18, f32[24,256]{1,0:T(8,128)S(1)} %add.344, pred[24]{0:T(512)(128)(4,1)S(1)} %get-tuple-element.638, bf16[24,16,256]{2,1,0:T(8,128)(2,1)S(1)} %bitcast.311, bf16[2,24,16,256]{3,2,1,0:T(8,128)(2,1)S(1)} %get-tuple-element.729, ...), kind=kOutput, calls=%fused_computation.43.clone.1 | convolution fusion | flops 72351744 | bytes 3588612 | tf_op jit(solution)/shard_map/while/body/eval_jaxpr/nda,ndb->nab/dot_general | solution.py:18
  261.9 1.5 fusion.121
  263.4 1.0 fusion.120
  264.8 5.1 %select_convert_fusion.5 = bf16[24,256,256]{2,1,0:T(8,128)(2,1)S(1)} fusion(f32[24,256]{1,0:T(8,128)S(1)} %multiply_reduce_fusion.18, f32[24,256]{1,0:T(8,128)S(1)} %add.344, pred[24]{0:T(512)(128)(4,1)S(1)} %get-tuple-element.638, bf16[24,16,256]{2,1,0:T(8,128)(2,1)S(1)} %bitcast.311, bf16[2,24,16,256]{3,2,1,0:T(8,128)(2,1)S(1)} %get-tuple-element.729, ...), kind=kOutput, calls=%fused_computation.43.clone.1 | convolution fusion | flops 72351744 | bytes 3588612 | tf_op jit(solution)/shard_map/while/body/eval_jaxpr/nda,ndb->nab/dot_general | solution.py:18
  270.0 1.5 fusion.121
  271.5 1.0 fusion.120
  272.8 5.1 %scatter_fusion.1 = f32[48,32,256]{2,1,0:T(8,128)S(1)} fusion(f32[48,32,256]{2,1,0:T(8,128)S(1)} %broadcast.415, s32[48]{0:T(128)S(1)} %fusion.62, f32[48,32,256]{2,1,0:T(8,128)} %bitcast.55), kind=kCustom, calls=%fused_computation.10 | custom fusion | bytes 4718784 | tf_op jit(solution)/shard_map/scatter | solution.py:86
  278.0 30.9 %all_to_all.36 = f32[8,6,32,256]{3,2,1,0:T(8,128)S(1)} all-to-all(f32[8,6,32,256]{3,2,1,0:T(8,128)S(1)} %bitcast.301), channel_id=1, replica_groups=mesh['rows'=8,'cols'=4] {'rows'}, dimensions={0} | all-to-all | bytes 3145728 | tf_op jit(solution)/shard_map/all_to_all | solution.py:88
  308.9 2.2 fusion.34
  311.2 30.6 %all-reduce.6.cloned.1.call-done = f32[8,32,256]{2,0,1:T(8,128)} async-done(((f32[8,32,256]{2,0,1:T(8,128)}), f32[8,32,256]{2,0,1:T(8,128)}) %all-reduce.6.cloned.1.call-update) | async-done | bytes 262160 | tf_op jit(solution)/shard_map/psum | solution.py:98
  341.8 1.5 multiply_reduce_fusion.6
  343.3 21.3 %psum.55 = f32[32]{0:T(128)S(1)} all-reduce(f32[32]{0:T(128)S(1)} %multiply_reduce_fusion.6), channel_id=1, replica_groups=mesh['rows'=8,'cols'=4] {'rows'}, use_global_device_ids=true, to_apply=%region_34.35 | all-reduce | flops 32 | bytes 256 | tf_op jit(solution)/shard_map/psum | solution.py:101
  364.6 1.1 multiply_subtract_fusion
  (128 shorter events, 15.0 us)
Async XLA Ops:
  11.4 13.8 %all-to-all-start = ((s32[8,6,2]{1,2,0:T(2,128)}), s32[8,6,2]{1,2,0:T(2,128)S(1)}, u32[]{:S(2)}, u32[]{:S(2)}) async-start(s32[8,6,2]{1,2,0:T(2,128)} %copy.20), calls=%async_computation | async-start | bytes 16384 | tf_op jit(solution)/shard_map/all_to_all | solution.py:54
  26.8 13.9 %all-to-all-start.1 = ((bf16[8,6,16,256]{3,2,1,0:T(8,128)(2,1)}), bf16[8,6,16,256]{3,2,1,0:T(8,128)(2,1)S(1)}, u32[]{:S(2)}, u32[]{:S(2)}) async-start(bf16[8,6,16,256]{3,2,1,0:T(8,128)(2,1)} %broadcast_select_fusion.5), calls=%async_computation.1 | async-start | bytes 786432 | tf_op jit(solution)/shard_map/all_to_all | solution.py:65
  41.4 17.6 %copy-start.1 = (f32[32,2048]{1,0:T(8,128)S(1)}, f32[32,2048]{1,0:T(8,128)}, u32[]{:S(2)}) copy-start(f32[32,2048]{1,0:T(8,128)} %param.11) | copy-start | bytes 786436
  55.4 10.5 %all-to-all-start.2 = ((f32[8,6,1,256]{3,2,1,0:T(1,128)}), f32[8,6,1,256]{3,2,1,0:T(1,128)S(1)}, u32[]{:S(2)}, u32[]{:S(2)}) async-start(f32[8,6,1,256]{3,2,1,0:T(1,128)} %reshape.520), calls=%async_computation.2 | async-start | bytes 98304 | tf_op jit(solution)/shard_map/all_to_all | solution.py:88
  73.6 23.9 %all-to-all-start.3 = ((bf16[8,6,32,256]{3,2,1,0:T(8,128)(2,1)}), bf16[8,6,32,256]{3,2,1,0:T(8,128)(2,1)S(1)}, u32[]{:S(2)}, u32[]{:S(2)}) async-start(bf16[8,6,32,256]{3,2,1,0:T(8,128)(2,1)} %broadcast_select_fusion.2), calls=%async_computation.3 | async-start | bytes 1572864 | tf_op jit(solution)/shard_map/all_to_all | solution.py:65
  77.1 117.9 %all-reduce.4.cloned.1.call-start = ((), (), s32[]{:S(2)}) async-start(), calls=%async_computation.7 | async-start | bytes 524288 | tf_op jit(solution)/shard_map/psum | solution.py:98
  163.8 178.0 %all-reduce.6.cloned.1.call-start = ((), (), s32[]{:S(2)}) async-start(), calls=%async_computation.8 | async-start | bytes 524288 | tf_op jit(solution)/shard_map/psum | solution.py:98
  278.0 63.8 %copy-start = (f32[8,32,256]{2,0,1:T(8,128)S(1)}, f32[8,32,256]{2,0,1:T(8,128)}, u32[]{:S(2)}) copy-start(f32[8,32,256]{2,0,1:T(8,128)} %all-reduce.4.cloned.1.call-done) | copy-start | bytes 786436
Sparse Core Ops, SparseCore 0:
  163.9 31.0 all-reduce.3
  311.3 30.4 all-reduce.5
where the time goes:
time: 375 us; the launch traced here: 374 us
  blocking collectives  153 us (41%)
  waiting for transfers between devices  104 us (28%)
  matrix products  47 us (13%)
  local copies, waits for them, and re-layouts  26.2 us (7%)
  starting transfers between devices  18 us (5%)
  between operations  14.4 us (4%)
  other arithmetic  10.7 us (3%)
    all_to_all x2, blocking collectives, give_back(): lax.all_to_all(placed.reshape(row_count, capacity, mirror.shape[1], block...  71.4 us
    psum x2, waiting for transfers between devices, column_total(): return lax.psum(partial_value, 'cols')  61.8 us
    psum x3, blocking collectives, global_sum(): return lax.psum(values, 'rows')  59.9 us
    dot_general x6, matrix products, wendland(): jnp.einsum('nda,ndb->nab', left_f, right_f, precision=lax.Precision.HIGHEST)  32.3 us
    all_to_all x2, waiting for transfers between devices, serve(): lax.all_to_all(chosen.reshape(row_count, capacity, blocks.shape[1], block...  29.9 us
    all_to_all x1, blocking collectives, serve(): lax.all_to_all(chosen.reshape(row_count, capacity, blocks.shape[1], block...  16.1 us
    scatter x3, local copies, waits for them, and re-layouts, give_back(): placed = jnp.zeros((buffer_len,) + mirror.shape[1:], jnp.float32).at[plac...  11 us
  transfers between devices with their start and end apart: 6, of which 6 were waited for; matrix products, arithmetic and copies ran while one was open for 0% of the time, Pallas kernels for 0%

commit v1 on v0

v1 whole, which is shorter than its diff:
```python
import functools

import jax
import jax.numpy as jnp
from jax import lax
from jax.experimental import pallas as pl
from jax.experimental.pallas import tpu as pltpu
from jax.sharding import PartitionSpec as P

REG = 1.5
RADIUS = 0.25
GROUP = 4
RING = 3
STRIP = 64
TINY = 1e-30
SHIFT = 0.375


def augment(x, first_ones):
    dim, n = x.shape
    norm = jnp.sum(x * x, axis=0, keepdims=True) / (RADIUS * RADIUS)
    high = norm.astype(jnp.bfloat16).astype(jnp.float32)
    rest = norm - high
    mid = rest.astype(jnp.bfloat16).astype(jnp.float32)
    low = rest - mid
    line = lax.broadcasted_iota(jnp.int32, (dim, n), 0)
    base = 3 if first_ones else 0
    ones_at = 0 if first_ones else 3
    tail = jnp.where((line >= ones_at) & (line < ones_at + 3), 1.0, 0.0)
    tail = jnp.where(line == base, high, tail)
    tail = jnp.where(line == base + 1, mid, tail)
    tail = jnp.where(line == base + 2, low, tail)
    return tail


def build_kernel(
    nb, block_len, own_rows, counts, own, x_ref, t_ref,
    k_hbm, jlist, groups, w_ref, inv_ref,
    mlist, kbuf, acc, lhs, sems,
):
    me = own[0]

    def copy_out(g):
        slot = lax.rem(g, RING)
        return pltpu.make_async_copy(kbuf.at[slot], k_hbm.at[g], sems.at[slot])

    ends = []
    pos = jnp.int32(0)
    for k in range(own_rows):

        def note(j, at, k=k):
            m = counts[k * nb + j]
            jlist[at] = j
            mlist[at] = m
            return at + jnp.where(m > 0, 1, 0)

        pos = lax.fori_loop(0, nb, note, pos, unroll=8)
        for u in range(GROUP):
            jlist[pos + u] = 0
            mlist[pos + u] = 0
        last = lax.div(pos + (GROUP - 1), GROUP)
        groups[k] = last
        ends.append(last)
        pos = last * GROUP

    scale = 1.0 / (RADIUS * RADIUS)
    for k in range(own_rows):
        begin = jnp.int32(0) if k == 0 else ends[k - 1]
        near = x_ref[me, :, k * block_len:(k + 1) * block_len].astype(jnp.float32)
        full = jnp.concatenate([near * (-2.0 * scale), augment(near, True)], axis=0)
        lhs[...] = full.T.astype(jnp.bfloat16)
        acc[...] = jnp.zeros_like(acc)

        def step(g, carry):
            slot = lax.rem(g, RING)

            @pl.when(g >= RING)
            def _():
                copy_out(g - RING).wait()

            for u in range(GROUP):
                j = jlist[g * GROUP + u]
                m = mlist[g * GROUP + u].astype(jnp.float32)
                dev = lax.div(j, own_rows)
                at = pl.multiple_of(lax.rem(j, own_rows) * block_len, block_len)
                far = x_ref[dev, :, pl.ds(at, block_len)]
                rhs = jnp.concatenate(
                    [far, augment(far.astype(jnp.float32), False).astype(jnp.bfloat16)], axis=0
                )
                for s in range(block_len // STRIP):
                    rows = slice(s * STRIP, (s + 1) * STRIP)
                    d = jnp.dot(lhs[rows, :], rhs, preferred_element_type=jnp.float32)
                    d = jnp.maximum(d, TINY)
                    sc = d * lax.rsqrt(d)
                    rem = jnp.maximum(1.0 - sc, 0.0)
                    sq = rem * rem
                    val = (sq * sq) * (sc * (4.0 * m) + m)
                    kbuf[slot, u, rows, :] = val.astype(jnp.bfloat16)
                    half = val[:, :128]
                    for h in range(1, block_len // 128):
                        half = half + val[:, h * 128:(h + 1) * 128]
                    acc[rows, :] += half
            copy_out(g).start()
            return carry

        lax.fori_loop(begin, ends[k], step, 0)
        degree = 1.0 + jnp.sum(acc[...].T, axis=0, keepdims=True)
        inv = 1.0 / jnp.sqrt(degree)
        cols = slice(k * block_len, (k + 1) * block_len)
        inv_ref[:, cols] = inv
        w_ref[:, cols] = (t_ref[:, cols] * inv).astype(jnp.bfloat16)

    def drain(g, carry):
        copy_out(g).wait()
        return carry

    lax.fori_loop(jnp.maximum(ends[-1] - RING, 0), ends[-1], drain, 0)


def apply_kernel(
    block_len, own_rows, first, jlist, groups, k_hbm, w_ref, inv_ref, prior_ref, *rest
):
    s_ref, kbuf, sems = rest[0], rest[-2], rest[-1]
    total = groups[own_rows - 1]

    def copy_in(g):
        slot = lax.rem(g, RING)
        return pltpu.make_async_copy(k_hbm.at[g], kbuf.at[slot], sems.at[slot])

    for p in range(RING - 1):

        @pl.when(p < total)
        def _(p=p):
            copy_in(p).start()

    for k in range(own_rows):
        begin = jnp.int32(0) if k == 0 else groups[k - 1]

        def step(g, acc):
            @pl.when(g + (RING - 1) < total)
            def _():
                copy_in(g + (RING - 1)).start()

            copy_in(g).wait()
            slot = lax.rem(g, RING)
            for u in range(GROUP):
                j = jlist[g * GROUP + u]
                dev = lax.div(j, own_rows)
                at = pl.multiple_of(lax.rem(j, own_rows) * block_len, block_len)
                acc = acc + lax.dot_general(
                    w_ref[dev, :, pl.ds(at, block_len)],
                    kbuf[slot, u],
                    (((1,), (1,)), ((), ())),
                    preferred_element_type=jnp.float32,
                )
            return acc

        acc = lax.fori_loop(begin, groups[k], step, jnp.zeros((s_ref.shape[0], block_len), jnp.float32))
        cols = slice(k * block_len, (k + 1) * block_len)
        inv = inv_ref[:, cols]
        s = acc * inv
        shift = SHIFT * prior_ref[:, cols]
        if first:
            s_ref[:, cols] = s
            rest[1][:, cols] = ((s - shift) * inv).astype(jnp.bfloat16)
        else:
            s_ref[:, cols] = s + shift


SMEM = pl.BlockSpec(memory_space=pltpu.SMEM)
VMEM = pl.BlockSpec(memory_space=pltpu.VMEM)
ANY = pl.BlockSpec(memory_space=pl.ANY)


def local(block_list, points, targets):
    n_rows = lax.axis_size("rows")
    n_cols = lax.axis_size("cols")
    row = lax.axis_index("rows")
    col = lax.axis_index("cols")
    block_rows, slots = block_list.shape
    dim, npoints = points.shape
    outputs = targets.shape[0]
    block_len = npoints // block_rows
    own_rows = block_rows // n_cols
    own_len = own_rows * block_len
    nb = block_rows * n_rows
    devices = n_rows * n_cols
    both = ("rows", "cols")
    capacity = -(-block_rows * slots // n_rows)
    bound = min(own_rows * nb, own_rows * slots * n_cols + devices * capacity)
    n_groups = -(-bound // GROUP) + own_rows
    me = row * n_cols + col

    own_points = lax.dynamic_slice_in_dim(points, col * own_len, own_len, 1)
    own_t = lax.dynamic_slice_in_dim(targets, col * own_len, own_len, 1)
    listed = jnp.pad(block_list + 1, ((0, 0), (0, 128 - slots)))
    coded = jnp.concatenate([listed // 32, listed % 32], axis=0).astype(jnp.bfloat16)
    packed = jnp.concatenate([own_points, coded], axis=1)
    gathered = lax.all_gather(packed, both, axis=0)
    codes = gathered[:, :, own_len:own_len + slots].astype(jnp.int32)
    entries = codes[:, :block_rows] * 32 + codes[:, block_rows:] - 1
    entries = entries.reshape(n_rows, n_cols, block_rows, slots)

    mine = me * own_rows + jnp.arange(own_rows, dtype=jnp.int32)
    names = jnp.arange(nb, dtype=jnp.int32)
    mirror = jnp.sum(
        (entries[None] == mine[:, None, None, None, None]).astype(jnp.int32), axis=(2, 4)
    ).reshape(own_rows, nb)
    own_entries = lax.dynamic_slice(
        entries, (row, 0, col * own_rows, 0), (1, n_cols, own_rows, slots)
    )[0].transpose(1, 0, 2).reshape(own_rows, n_cols * slots)
    direct = jnp.sum((own_entries[:, :, None] == names).astype(jnp.int32), axis=1)
    counts = direct + jnp.where(names[None, :] == mine[:, None], 0, mirror)

    k_mat, jlist, groups, w1, inv = pl.pallas_call(
        functools.partial(build_kernel, nb, block_len, own_rows),
        out_shape=(
            jax.ShapeDtypeStruct((n_groups, GROUP, block_len, block_len), jnp.bfloat16),
            jax.ShapeDtypeStruct(((n_groups + 1) * GROUP,), jnp.int32),
            jax.ShapeDtypeStruct((own_rows,), jnp.int32),
            jax.ShapeDtypeStruct((outputs, own_len), jnp.bfloat16),
            jax.ShapeDtypeStruct((1, own_len), jnp.float32),
        ),
        in_specs=[SMEM, SMEM, VMEM, VMEM],
        out_specs=(ANY, SMEM, SMEM, VMEM, VMEM),
        scratch_shapes=[
            pltpu.SMEM(((n_groups + 1) * GROUP,), jnp.int32),
            pltpu.VMEM((RING, GROUP, block_len, block_len), jnp.bfloat16),
            pltpu.VMEM((block_len, 128), jnp.float32),
            pltpu.VMEM((block_len, 2 * dim), jnp.bfloat16),
            pltpu.SemaphoreType.DMA((RING,)),
        ],
        compiler_params=pltpu.CompilerParams(vmem_limit_bytes=32 * 1024 * 1024),
        name="build",
    )(counts.reshape(own_rows * nb), me.reshape(1), gathered, own_t)

    def apply(first, w_all, prior):
        shapes = [
            jax.ShapeDtypeStruct((outputs, own_len), jnp.float32),
            jax.ShapeDtypeStruct((outputs, own_len), jnp.bfloat16),
        ]
        return pl.pallas_call(
            functools.partial(apply_kernel, block_len, own_rows, first),
            out_shape=shapes if first else shapes[:1],
            in_specs=[SMEM, SMEM, ANY, VMEM, VMEM, VMEM],
            out_specs=[VMEM, VMEM] if first else [VMEM],
            scratch_shapes=[
                pltpu.VMEM((RING, GROUP, block_len, block_len), jnp.bfloat16),
                pltpu.SemaphoreType.DMA((RING,)),
            ],
            compiler_params=pltpu.CompilerParams(vmem_limit_bytes=32 * 1024 * 1024),
            name="apply",
        )(jlist, groups, k_mat, w_all, inv, prior)

    s1, q1 = apply(True, lax.all_gather(w1, both, axis=0), own_t)
    (s2,) = apply(False, lax.all_gather(q1, both, axis=0), s1)

    pairs = jnp.stack(
        [
            jnp.sum(own_t * own_t, axis=1),
            jnp.sum(own_t * s1, axis=1),
            jnp.sum(s1 * s1, axis=1),
            jnp.sum(own_t * s2, axis=1),
            jnp.sum(s1 * s2, axis=1),
        ]
    )
    tt, ts1, s1s1, ts2, s1s2 = lax.psum(pairs, both)
    spread = lax.all_gather(jnp.stack([s1, s2]), "cols", axis=2, tiled=False)
    wide = spread.reshape(2, outputs, npoints)
    s1w, s2w = wide[0], wide[1]

    a1 = tt / (REG * tt + ts1)
    p = 1.0 - REG * a1
    new = p * p * tt - 2.0 * p * a1 * ts1 + a1 * a1 * s1s1
    u = p + new / tt
    dd = u * u * tt - 2.0 * u * a1 * ts1 + a1 * a1 * s1s1
    dmd = u * u * ts1 - u * a1 * (s1s1 + ts2) + a1 * a1 * s1s2
    a2 = new / (REG * dd + dmd)
    c = lambda v: v[:, None]
    sol = c(a1 + a2 * u) * targets - c(a2 * a1) * s1w
    res = (
        c(p - a2 * REG * u) * targets
        + c(-a1 - a2 * (u - REG * a1)) * s1w
        + c(a2 * a1) * s2w
    )
    return (sol, res)


def solution(mesh):
    placed = (P("rows", "cols"), P(None, "rows"), P(None, "rows"))
    return jax.shard_map(
        local,
        mesh=mesh,
        in_specs=placed,
        out_specs=(P(None, "rows"), P(None, "rows")),
        check_vma=False,
    )
```

time: 375 us -> 251 us (0.67)
  blocking collectives: 153 us -> 91.6 us
  matrix products: 47 us -> 0 us
  starting transfers between devices: 18 us -> 0.08 us
  Pallas kernels: 0 us -> 17.8 us
  other arithmetic: 10.7 us -> 2.25 us
  local copies, waits for them, and re-layouts: 26.2 us -> 22.2 us
    all_gather x0 -> x2, waiting for transfers between devices: none -> 102 us  [the longest x1 52.5 us: local(): s2, = apply(False, lax.all_gather(q1, both, axis=0), s1)]
    all_to_all x3 -> x0, blocking collectives: 87.5 us -> none  [the longest x2 71.4 us: give_back(): lax.all_to_all(placed.reshape(row_count, capacity, mirror.shape[1], block...]
    psum x2 -> x0, waiting for transfers between devices: 61.8 us -> none  [column_total(): return lax.psum(partial_value, 'cols')]
    all_gather x0 -> x2, blocking collectives: none -> 53 us  [the longest x1 45 us: local(): gathered = lax.all_gather(packed, both, axis=0)]
    dot_general x17 -> x0, matrix products: 47 us -> none  [the longest x6 32.3 us: wendland(): jnp.einsum('nda,ndb->nab', left_f, right_f, precision=lax.Precision.HIGHEST)]
    all_to_all x4 -> x0, waiting for transfers between devices: 42.3 us -> none  [the longest x2 29.9 us: serve(): lax.all_to_all(chosen.reshape(row_count, capacity, blocks.shape[1], block...]
    psum x4 -> x1, blocking collectives: 65.7 us -> 38.7 us  [local(): tt, ts1, s1s1, ts2, s1s2 = lax.psum(pairs, both)]
    unnamed x7 -> x14, local copies, waits for them, and re-layouts: 1.67 us -> 20.7 us
  transfers between devices with their start and end apart: 6 -> 2, of which waited for: 6 -> 2; matrix products, arithmetic and copies ran while one was open for 0% -> 0% of each run, Pallas kernels for 0% -> 0%
where the time goes in v1:
time: 251 us; the launch traced here: 250 us
  waiting for transfers between devices  102 us (41%)
  blocking collectives  91.6 us (36%)
  local copies, waits for them, and re-layouts  22.2 us (9%)
  Pallas kernels  17.8 us (7%)
  between operations  14.2 us (6%)
    all_gather x1, waiting for transfers between devices, local(): s2, = apply(False, lax.all_gather(q1, both, axis=0), s1)  52.5 us
    all_gather x1, waiting for transfers between devices, local(): s1, q1 = apply(True, lax.all_gather(w1, both, axis=0), own_t)  49.8 us
    all_gather x1, blocking collectives, local(): gathered = lax.all_gather(packed, both, axis=0)  45 us
    psum x1, blocking collectives, local(): tt, ts1, s1s1, ts2, s1s2 = lax.psum(pairs, both)  38.7 us
    unnamed x14, local copies, waits for them, and re-layouts  20.7 us
    pallas_call x1, Pallas kernels, local(): pl.pallas_call(functools.partial(build_kernel, nb, block_len, own_rows),...  9.2 us
    pallas_call x2, Pallas kernels, apply(): pl.pallas_call(functools.partial(apply_kernel, block_len, own_rows, first...  8.62 us
    all_gather x1, blocking collectives, local(): spread = lax.all_gather(jnp.stack([s1, s2]), 'cols', axis=2, tiled=False)  7.95 us
  transfers between devices with their start and end apart: 2, of which 2 were waited for; matrix products, arithmetic and copies ran while one was open for 0% of the time, Pallas kernels for 0%

profile of v1, /device:TPU:0, one launch (start us, length us, event | category | flops | bytes accessed | tf_op | source)
XLA Modules:
  0.0 250.5 jit_solution(4504694914059569834)
XLA Ops:
  7.2 0.0 copy-start
  7.2 0.0 all-gather.7.cloned.1.call-start
  7.2 0.1 iota_compare_fusion.1
  7.3 0.1 eq.54
  7.4 0.7 broadcast_add_fusion
  8.1 0.0 copy-done
  8.1 0.9 constant_dynamic-slice_fusion.1.t_ref.prior_ref
  9.0 45.0 %all-gather = bf16[512,640]{1,0:T(8,128)(2,1)S(1)} all-gather(bf16[16,640]{1,0:T(8,128)(2,1)S(1)} %maximum_maximum_fusion), channel_id=2, replica_groups=mesh['rows'=8,'cols'=4] {'rows','cols'}, dimensions={0}, use_global_device_ids=true | all-gather | bytes 675840 | tf_op jit(solution)/shard_map/all_gather | solution.py:199
  54.1 0.3 copy.7
  54.3 0.1 convert_reduce_fusion
  54.5 0.1 reshape.215
  54.6 0.1 eq.47
  54.7 0.1 convert_reduce_fusion.1
  54.8 0.1 reduce_sum.67
  54.8 9.2 %build.1 = (bf16[34,4,256,256]{3,2,1,0:T(8,128)(2,1)S(1)}, s32[140]{0:T(256)S(1)}, s32[2]{0:T(128)S(1)}, bf16[32,512]{1,0:T(8,128)(2,1)}, f32[1,512]{1,0:T(1,128)S(1)}) custom-call(s32[128]{0:T(128)S(1)} %select_add_fusion.counts, s32[1]{0:T(128)} %bitcast.5.own, bf16[32,16,640]{2,1,0:T(8,128)(2,1)S(1)} %bitcast.95, ...), custom_call_target="tpu_custom_call" | custom-call | tf_op jit(solution)/shard_map/build/pallas_call | solution.py:215
  64.1 0.0 copy-start.1
  64.1 6.1 %copy-done.1 = bf16[34,4,256,256]{3,2,1,0:T(8,128)(2,1)} copy-done((bf16[34,4,256,256]{3,2,1,0:T(8,128)(2,1)}, bf16[34,4,256,256]{3,2,1,0:T(8,128)(2,1)S(1)}, u32[]{:S(2)}) %copy-start.1) | copy-done | bytes 17825816
  70.2 0.0 all-gather.7.cloned.1.call-update
  70.2 0.0 all-gather.9.cloned.1.call-start
  70.3 49.8 %all-gather.7.cloned.1.call-done = bf16[1024,512]{1,0:T(8,128)(2,1)} async-done(((bf16[32,512]{1,0:T(8,128)(2,1)}), bf16[1024,512]{1,0:T(8,128)(2,1)}) %all-gather.7.cloned.1.call-update) | async-done | bytes 1048592 | tf_op jit(solution)/shard_map/all_gather | solution.py:255
  120.0 0.0 copy-start.2
  120.0 6.1 %copy-done.2 = bf16[34,4,256,256]{3,2,1,0:T(8,128)(2,1)S(1)} copy-done((bf16[34,4,256,256]{3,2,1,0:T(8,128)(2,1)S(1)}, bf16[34,4,256,256]{3,2,1,0:T(8,128)(2,1)}, u32[]{:S(2)}) %copy-start.2) | copy-done | bytes 17825816
  126.1 0.0 copy-start.4
  126.1 1.2 copy-done.4
  127.3 0.0 copy-start.6
  127.3 4.6 %apply.2 = (f32[32,512]{1,0:T(8,128)S(1)}, bf16[32,512]{1,0:T(8,128)(2,1)}) custom-call(s32[140]{0:T(256)S(1)} %get-tuple-element.9.jlist, s32[2]{0:T(128)S(1)} %get-tuple-element.10.groups, bf16[34,4,256,256]{3,2,1,0:T(8,128)(2,1)S(1)} %copy-done.2, bf16[32,32,512]{2,1,0:T(8,128)(2,1)S(1)} %bitcast.96, f32[1,512]{1,0:T(1,128)S(1)} %get-tuple-element.13.inv_ref, ...), custom_call_target="tpu_custom_call" | custom-call | tf_op jit(solution)/shard_map/apply/pallas_call | solution.py:242
  131.9 0.0 all-gather.9.cloned.1.call-update
  132.0 52.5 %all-gather.9.cloned.1.call-done = bf16[1024,512]{1,0:T(8,128)(2,1)} async-done(((bf16[32,512]{1,0:T(8,128)(2,1)}), bf16[1024,512]{1,0:T(8,128)(2,1)}) %all-gather.9.cloned.1.call-update) | async-done | bytes 1048592 | tf_op jit(solution)/shard_map/all_gather | solution.py:256
  184.5 0.0 copy-start.3
  184.5 6.1 %copy-done.3 = bf16[34,4,256,256]{3,2,1,0:T(8,128)(2,1)S(1)} copy-done((bf16[34,4,256,256]{3,2,1,0:T(8,128)(2,1)S(1)}, bf16[34,4,256,256]{3,2,1,0:T(8,128)(2,1)}, u32[]{:S(2)}) %copy-start.3) | copy-done | bytes 17825816
  190.5 0.0 copy-start.5
  190.5 1.2 copy-done.5
  191.8 4.0 %apply.3 = f32[32,512]{1,0:T(8,128)S(1)} custom-call(s32[140]{0:T(256)S(1)} %get-tuple-element.9.jlist, s32[2]{0:T(128)S(1)} %get-tuple-element.10.groups, bf16[34,4,256,256]{3,2,1,0:T(8,128)(2,1)S(1)} %copy-done.3, bf16[32,32,512]{2,1,0:T(8,128)(2,1)S(1)} %bitcast.97, f32[1,512]{1,0:T(1,128)S(1)} %get-tuple-element.13.inv_ref, ...), custom_call_target="tpu_custom_call" | custom-call | tf_op jit(solution)/shard_map/apply/pallas_call | solution.py:242
  195.8 0.0 copy-done.6
  195.8 0.2 multiply_reduce_fusion
  196.0 38.7 %psum.7 = f32[5,32]{1,0:T(8,128)S(1)} all-reduce(f32[5,32]{1,0:T(8,128)S(1)} %stack.32), channel_id=1, replica_groups=mesh['rows'=8,'cols'=4] {'rows','cols'}, use_global_device_ids=true, to_apply=%region_7.8 | all-reduce | flops 160 | bytes 1280 | tf_op jit(solution)/shard_map/psum | solution.py:267
  234.7 8.0 %all-gather.3 = f32[2,32,2048]{2,1,0:T(8,128)S(1)} all-gather(f32[2,32,512]{2,1,0:T(8,128)S(1)} %pad_maximum_fusion), channel_id=5, replica_groups=mesh['rows'=8,'cols'=4] {'cols'}, dimensions={2}, use_global_device_ids=true | all-gather | bytes 655360 | tf_op jit(solution)/shard_map/all_gather | solution.py:268
  242.7 1.0 fusion.1
  (14 shorter events, 0.2 us)
Async XLA Ops:
  7.2 1.0 copy-start
  7.2 112.8 %all-gather.7.cloned.1.call-start = ((), (), s32[]{:S(2)}) async-start(), calls=%async_computation | async-start | bytes 1081344 | tf_op jit(solution)/shard_map/all_gather | solution.py:255
  64.1 6.1 %copy-start.1 = (bf16[34,4,256,256]{3,2,1,0:T(8,128)(2,1)}, bf16[34,4,256,256]{3,2,1,0:T(8,128)(2,1)S(1)}, u32[]{:S(2)}) copy-start(bf16[34,4,256,256]{3,2,1,0:T(8,128)(2,1)S(1)} %get-tuple-element.11.k_hbm) | copy-start | bytes 53477380
  70.2 114.3 %all-gather.9.cloned.1.call-start = ((), (), s32[]{:S(2)}) async-start(), calls=%async_computation.1 | async-start | bytes 1081344 | tf_op jit(solution)/shard_map/all_gather | solution.py:256
  120.0 6.1 %copy-start.2 = (bf16[34,4,256,256]{3,2,1,0:T(8,128)(2,1)S(1)}, bf16[34,4,256,256]{3,2,1,0:T(8,128)(2,1)}, u32[]{:S(2)}) copy-start(bf16[34,4,256,256]{3,2,1,0:T(8,128)(2,1)} %copy-done.1) | copy-start | bytes 53477380
  126.1 1.2 copy-start.4
  127.3 68.5 %copy-start.6 = (f32[32,2048]{1,0:T(8,128)S(1)}, f32[32,2048]{1,0:T(8,128)}, u32[]{:S(2)}) copy-start(f32[32,2048]{1,0:T(8,128)} %param.5) | copy-start | bytes 786436
  184.5 6.1 %copy-start.3 = (bf16[34,4,256,256]{3,2,1,0:T(8,128)(2,1)S(1)}, bf16[34,4,256,256]{3,2,1,0:T(8,128)(2,1)}, u32[]{:S(2)}) copy-start(bf16[34,4,256,256]{3,2,1,0:T(8,128)(2,1)} %copy-done.1) | copy-start | bytes 53477380
  190.5 1.2 copy-start.5
Sparse Core Ops, SparseCore 0:
  70.3 49.6 all-gather.6
  132.1 52.3 all-gather.8
